TPU v7x, 256 devices: a whole 4x4x8 slice. The times are simulated.
256 devices in a mesh: seq: 64 (over z_hi, y, x), red: 4 (over z_lo, core).
Axes of the slice: x: 4, y: 4, z: 8 (z_hi: 4, z_lo: 2; z = z_hi * 2 + z_lo), core: 2. Of those that a mesh axis runs over, the one named last changes fastest.
Arguments:
- token_ids: int32 [8192], P('seq'), may hold values from 0 to 511
- embedding: bfloat16 [512, 4096], P(None, 'red'), may hold values from -6 to 6
- proj_weight: bfloat16 [4096, 3, 4, 256], P('red', None, None, 'seq'), may hold values from -0.09375 to 0.09375
- filters: float32 [8192, 1024], P('seq', 'red'), may hold values from -1 to 1
- cotangent: float32 [8192, 1024], P('seq', 'red'), may hold values from -6 to 6
Outputs:
- output: float32 [8192, 1024], P('seq', 'red')
- filter_grad: float32 [8192, 1024], P('seq', 'red')
- branch_grads: bfloat16 [8192, 3, 1024], P('seq', None, 'red')
- weight_grad: float32 [4096, 3, 4, 256], P('red', None, None, 'seq')
All inputs are finite; a program needn't handle non-finite values.
Results may differ from a plain program's by a relative error of at most 0.0029.
Values sent between devices are 32-bit elements; how exact they have to be, the bound alone decides.
No kernel may reach another device: no remote copies, remote signals or barrier semaphores. Data moves between devices by JAX's collectives and lax.ppermute only.
A program may use at most 64 MiB of HBM per device.

v0:
```python
import math
import jax
import jax.numpy as jnp
from jax import lax
from jax.sharding import PartitionSpec as P

precise_mode = lax.Precision.HIGHEST


def in_blocks(value, dim, length):
    before, after = (value.shape[:dim], value.shape[dim + 1 :])
    return jnp.moveaxis(value.reshape(*before, length, -1, *after), dim, 0)


def summed_on_arrival(value, axis, dim):
    tiles = in_blocks(value, dim, lax.axis_size(axis))
    arrived = lax.all_to_all(tiles, axis, split_axis=0, concat_axis=0, tiled=True)
    return arrived.sum(axis=0)


def copy_for_each(value, axis):
    length = lax.axis_size(axis)
    return lax.all_to_all(
        jnp.broadcast_to(value[None], (length, *value.shape)), axis, 0, 0, tiled=True
    )


def in_order(tiles, dim):
    tiles = jnp.moveaxis(tiles, 0, dim)
    shape = tiles.shape
    return tiles.reshape(*shape[:dim], shape[dim] * shape[dim + 1], *shape[dim + 2 :])


def gather_directly(value, axis, dim):
    tiles = copy_for_each(value, axis)
    return in_order(tiles, dim)


def angles(numbers, modulus, direction):
    phase = (numbers % modulus).astype(jnp.float32) * (direction * 2.0 * math.pi / modulus)
    return (jnp.cos(phase), jnp.sin(phase))


def rotate(real_part, imag_part, cosine, sine_part):
    return (real_part * cosine - imag_part * sine_part, real_part * sine_part + imag_part * cosine)


def complex_einsum(formula, matrix, values):
    mat_real, mat_imag = matrix
    val_real, val_imag = values
    real_out = jnp.einsum(formula, mat_real, val_real, precision=precise_mode) - jnp.einsum(
        formula, mat_imag, val_imag, precision=precise_mode
    )
    imag_out = jnp.einsum(formula, mat_real, val_imag, precision=precise_mode) + jnp.einsum(
        formula, mat_imag, val_real, precision=precise_mode
    )
    return (real_out, imag_out)


def factors(length_total):
    first_factor = 1
    for candidate in range(1, math.isqrt(length_total) + 1):
        if length_total % candidate == 0:
            first_factor = candidate
    return (first_factor, length_total // first_factor)


def combine_spectra(spec_real, spec_imag, width):
    filt_re = spec_real[..., :width]
    inner_re = spec_real[..., width : 2 * width]
    up_re = spec_real[..., 2 * width :]
    filt_im = spec_imag[..., :width]
    inner_im = spec_imag[..., width : 2 * width]
    up_im = spec_imag[..., 2 * width :]
    joined_real = jnp.concatenate(
        [
            filt_re * inner_re - filt_im * inner_im,
            filt_re * up_re + filt_im * up_im,
            up_re * inner_re + up_im * inner_im,
        ],
        axis=-1,
    )
    joined_imag = jnp.concatenate(
        [
            filt_re * inner_im + filt_im * inner_re,
            filt_re * up_im - filt_im * up_re,
            up_im * inner_re - up_re * inner_im,
        ],
        axis=-1,
    )
    return (joined_real, joined_imag)


def local_convolve(signals):
    length, branch_count, narrow = signals.shape
    total = 2 * length
    first_factor, second_factor = factors(total)
    flat = signals.reshape(length, branch_count * narrow)
    padded = jnp.concatenate([flat, jnp.zeros_like(flat)], axis=0).reshape(
        first_factor, second_factor, branch_count * narrow
    )
    first_index = jnp.arange(first_factor, dtype=jnp.int32)
    second_index = jnp.arange(second_factor, dtype=jnp.int32)
    cosine, sine_part = angles(first_index[:, None] * first_index[None, :], first_factor, -1.0)
    real_part = jnp.einsum("kn,nbm->kbm", cosine, padded, precision=precise_mode)
    imag_part = jnp.einsum("kn,nbm->kbm", sine_part, padded, precision=precise_mode)
    cosine, sine_part = angles(first_index[:, None] * second_index[None, :], total, -1.0)
    real_part, imag_part = rotate(real_part, imag_part, cosine[:, :, None], sine_part[:, :, None])
    real_part, imag_part = complex_einsum(
        "lb,kbm->klm",
        angles(second_index[:, None] * second_index[None, :], second_factor, -1.0),
        (real_part, imag_part),
    )
    real_part, imag_part = combine_spectra(real_part, imag_part, narrow)
    real_part, imag_part = complex_einsum(
        "bl,klm->kbm",
        angles(second_index[:, None] * second_index[None, :], second_factor, 1.0),
        (real_part, imag_part),
    )
    cosine, sine_part = angles(first_index[:, None] * second_index[None, :], total, 1.0)
    real_part, imag_part = rotate(real_part, imag_part, cosine[:, :, None], sine_part[:, :, None])
    cosine, sine_part = angles(first_index[:, None] * first_index[None, :], first_factor, 1.0)
    result = jnp.einsum("nk,kbm->nbm", cosine, real_part, precision=precise_mode) - jnp.einsum(
        "nk,kbm->nbm", sine_part, imag_part, precision=precise_mode
    )
    result = result.reshape(total, branch_count * narrow)[:length] / total
    return result.reshape(length, branch_count, narrow)


def shards(token_ids, embedding, proj_weight, filters, cotangent):
    tok_count = token_ids.shape[0]
    devices = lax.axis_size("seq")
    width = filters.shape[1]
    vocabulary = embedding.shape[0]
    width_rows, branches, red_count, piece = proj_weight.shape
    scale_factor = float(tok_count * devices) ** (-0.5)
    table = jnp.dot(
        embedding,
        proj_weight.reshape(width_rows, branches * red_count * piece),
        preferred_element_type=jnp.float32,
    )
    table = table.reshape(vocabulary, branches, red_count, piece)
    own_table = summed_on_arrival(table, "red", 2)
    full_table = gather_directly(own_table, "seq", 3)
    projected = jnp.take(full_table, token_ids, axis=0)
    projected = projected.reshape(tok_count, branches, width)
    queries = projected[:, 0]
    key_rows = projected[:, 1]
    value_rows = projected[:, 2]
    inner = key_rows * value_rows
    upstream = cotangent * queries
    stacked = jnp.stack([filters, inner, upstream], axis=1)
    whole_length = lax.all_to_all(stacked, "seq", split_axis=2, concat_axis=0, tiled=True)
    results = local_convolve(whole_length)
    returned = lax.all_to_all(results, "seq", split_axis=0, concat_axis=2, tiled=True)
    conv = returned[:, 0]
    grad_inner = returned[:, 1]
    filter_raw = returned[:, 2]
    output = queries * conv
    filter_grad = filter_raw * scale_factor
    branch_grads = jnp.stack(
        [cotangent * conv, grad_inner * value_rows, grad_inner * key_rows], axis=1
    ).astype(jnp.bfloat16)
    one_hot = (token_ids[:, None] == lax.iota(jnp.int32, vocabulary)[None, :]).astype(jnp.bfloat16)
    token_sums = lax.dot_general(
        one_hot,
        branch_grads.reshape(tok_count, branches * width),
        (((0,), (0,)), ((), ())),
        preferred_element_type=jnp.float32,
    )
    summed = summed_on_arrival(token_sums.reshape(vocabulary, branches, width), "seq", 2)
    gathered = gather_directly(summed[:, :, None, :], "red", 2)
    weight_grad = (
        lax.dot_general(
            embedding.astype(jnp.float32),
            gathered.reshape(vocabulary, branches * red_count * piece),
            (((0,), (0,)), ((), ())),
            precision=precise_mode,
        )
        * scale_factor
    )
    return (
        output,
        filter_grad,
        branch_grads,
        weight_grad.reshape(width_rows, branches, red_count, piece),
    )


def solution(mesh):
    in_specs = (
        P("seq"),
        P(None, "red"),
        P("red", None, None, "seq"),
        P("seq", "red"),
        P("seq", "red"),
    )
    out_specs = (
        P("seq", "red"),
        P("seq", "red"),
        P("seq", None, "red"),
        P("red", None, None, "seq"),
    )
    return jax.shard_map(shards, mesh=mesh, in_specs=in_specs, out_specs=out_specs, check_vma=False)
```

profile of v0, /device:TPU:1, one launch (start us, length us, event | category | flops | bytes accessed | tf_op | source)
XLA Modules:
  0.0 240.9 jit_solution(10747169346815855003)
XLA Ops:
  2.4 9.0 %all_to_all.53 = f32[4,512,3,1,4]{1,4,2,3,0:T(4,128)S(1)} all-to-all(f32[4,512,3,1,4]{1,4,2,3,0:T(4,128)S(1)} %copy.50), channel_id=1, replica_groups=mesh['seq'=64,'red'=4] {'red'}, dimensions={0} | all-to-all | bytes 196608 | tf_op jit(solution)/shard_map/all_to_all | solution.py:17
  11.4 1.4 broadcast_in_dim.17
  12.7 12.7 %all-to-all-start.1 = ((f32[64,512,3,1,4]{1,4,2,3,0:T(4,128)}), f32[64,512,3,1,4]{1,4,2,3,0:T(4,128)S(1)}, u32[]{:S(2)}, u32[]{:S(2)}) async-start(f32[64,512,3,1,4]{1,4,2,3,0:T(4,128)} %broadcast_in_dim.17), calls=%async_computation.1 | async-start | bytes 3145728 | tf_op jit(solution)/shard_map/all_to_all | solution.py:23
  25.6 39.4 %all-to-all-done.1 = f32[64,512,3,1,4]{1,4,2,3,0:T(4,128)S(1)} async-done(((f32[64,512,3,1,4]{1,4,2,3,0:T(4,128)}), f32[64,512,3,1,4]{1,4,2,3,0:T(4,128)S(1)}, u32[]{:S(2)}, u32[]{:S(2)}) %all-to-all-start.1) | async-done | bytes 1572896 | tf_op jit(solution)/shard_map/all_to_all | solution.py:23
  65.0 1.5 copy.51
  66.5 1.8 reshape.123
  68.3 1.8 copy.52
  70.1 2.5 %gather_fusion = f32[128,3,256]{2,1,0:T(4,128)S(1)} fusion(f32[512,3,256]{2,1,0:T(4,128)} %copy.52, s32[1024]{0:T(1024)S(1)} %pad_clamp_fusion), kind=kCustom, calls=%fused_computation | custom fusion | bytes 786944 | tf_op jit(solution)/shard_map/jit(_take)/gather | solution.py:145
  74.6 8.6 %all-to-all-start.2 = ((f32[128,3,256]{0,1,2:T(4,128)}), f32[128,3,256]{0,1,2:T(4,128)S(1)}, u32[]{:S(2)}, u32[]{:S(2)}) async-start(f32[128,3,256]{0,1,2:T(4,128)} %copy.54), calls=%async_computation.2 | async-start | bytes 1048576 | tf_op jit(solution)/shard_map/all_to_all | solution.py:153
  83.8 14.8 %all-to-all-done.2 = f32[128,3,256]{0,1,2:T(4,128)S(1)} async-done(((f32[128,3,256]{0,1,2:T(4,128)}), f32[128,3,256]{0,1,2:T(4,128)S(1)}, u32[]{:S(2)}, u32[]{:S(2)}) %all-to-all-start.2) | async-done | bytes 393248 | tf_op jit(solution)/shard_map/all_to_all | solution.py:153
  99.4 1.1 fusion.4
  110.0 1.3 fusion.10
  111.4 1.1 fusion.8
  112.7 10.7 %copy.57 = f32[8192,3,4]{2,1,0:T(4,128)} copy(f32[8192,3,4]{0,2,1:T(4,128)S(1)} %div.10) | data formatting | bytes 786432 | tf_op jit(solution)/shard_map/div | solution.py:126
  123.3 16.0 %reshape.142 = f32[64,1,1536]{2,1,0:T(1,128)S(1)} reshape(f32[8192,3,4]{2,1,0:T(4,128)} %copy.57) | data formatting | bytes 786432
  139.4 19.7 %all_to_all.54 = f32[64,1,1536]{2,1,0:T(1,128)S(1)} all-to-all(f32[64,1,1536]{2,1,0:T(1,128)S(1)} %reshape.142), channel_id=1, replica_groups=mesh['seq'=64,'red'=4] {'seq'}, dimensions={0} | all-to-all | bytes 786432 | tf_op jit(solution)/shard_map/all_to_all | solution.py:155
  159.6 1.6 reduce.1
  161.1 11.5 %reshape.143 = f32[8192,3,4]{2,1,0:T(4,128)} reshape(f32[64,1536]{1,0:T(8,128)S(1)} %reduce.1) | data formatting | bytes 786432
  172.6 11.7 %copy.58 = f32[64,128,3,4]{1,3,0,2:T(4,128)S(1)} copy(f32[64,128,3,4]{3,2,1,0:T(4,128)} %bitcast.114) | data formatting | bytes 786432 | tf_op jit(solution)/shard_map/all_to_all | solution.py:155
  186.2 2.2 copy.64
  188.4 5.3 %all-to-all-start.4 = ((f32[64,512,3,4]{1,3,2,0:T(4,128)}), f32[64,512,3,4]{1,3,2,0:T(4,128)S(1)}, u32[]{:S(2)}, u32[]{:S(2)}) async-start(f32[64,512,3,4]{1,3,2,0:T(4,128)} %copy.64), calls=%async_computation.4 | async-start | bytes 3145728 | tf_op jit(solution)/shard_map/all_to_all | solution.py:17
  195.2 27.0 %all-to-all-done.4 = f32[64,512,3,4]{1,3,2,0:T(4,128)S(1)} async-done(((f32[64,512,3,4]{1,3,2,0:T(4,128)}), f32[64,512,3,4]{1,3,2,0:T(4,128)S(1)}, u32[]{:S(2)}, u32[]{:S(2)}) %all-to-all-start.4) | async-done | bytes 1572896 | tf_op jit(solution)/shard_map/all_to_all | solution.py:17
  223.0 13.1 %all-to-all-start.5 = ((f32[4,512,3,1,4]{1,4,2,3,0:T(4,128)}), f32[4,512,3,1,4]{1,4,2,3,0:T(4,128)S(1)}, u32[]{:S(2)}, u32[]{:S(2)}) async-start(f32[4,512,3,1,4]{1,4,2,3,0:T(4,128)} %broadcast_in_dim.20), calls=%async_computation.5 | async-start | bytes 196608 | tf_op jit(solution)/shard_map/all_to_all | solution.py:23
  236.8 2.7 %all-to-all-done.5 = f32[4,512,3,1,4]{1,4,2,3,0:T(4,128)S(1)} async-done(((f32[4,512,3,1,4]{1,4,2,3,0:T(4,128)}), f32[4,512,3,1,4]{1,4,2,3,0:T(4,128)S(1)}, u32[]{:S(2)}, u32[]{:S(2)}) %all-to-all-start.5) | async-done | bytes 98336 | tf_op jit(solution)/shard_map/all_to_all | solution.py:23
  (63 shorter events, 21.5 us)
Async XLA Ops:
  0.6 1.3 copy-start
  12.7 12.7 %copy-start.2 = (f32[128,256]{1,0:T(8,128)S(1)}, f32[128,256]{1,0:T(8,128)}, u32[]{:S(2)}) copy-start(f32[128,256]{1,0:T(8,128)} %param.8) | copy-start | bytes 393220
  12.7 12.8 %copy-start.3 = (s32[128]{0:T(128)S(1)}, s32[128]{0:T(128)}, u32[]{:S(2)}) copy-start(s32[128]{0:T(128)} %param.5) | copy-start | bytes 1540
  12.7 52.2 %all-to-all-start.1 = ((f32[64,512,3,1,4]{1,4,2,3,0:T(4,128)}), f32[64,512,3,1,4]{1,4,2,3,0:T(4,128)S(1)}, u32[]{:S(2)}, u32[]{:S(2)}) async-start(f32[64,512,3,1,4]{1,4,2,3,0:T(4,128)} %broadcast_in_dim.17), calls=%async_computation.1 | async-start | bytes 3145728 | tf_op jit(solution)/shard_map/all_to_all | solution.py:23
  70.1 3.0 %copy-start.1 = (f32[128,256]{1,0:T(8,128)S(1)}, f32[128,256]{1,0:T(8,128)}, u32[]{:S(2)}) copy-start(f32[128,256]{1,0:T(8,128)} %param.9) | copy-start | bytes 393220
  74.6 24.1 %all-to-all-start.2 = ((f32[128,3,256]{0,1,2:T(4,128)}), f32[128,3,256]{0,1,2:T(4,128)S(1)}, u32[]{:S(2)}, u32[]{:S(2)}) async-start(f32[128,3,256]{0,1,2:T(4,128)} %copy.54), calls=%async_computation.2 | async-start | bytes 1048576 | tf_op jit(solution)/shard_map/all_to_all | solution.py:153
  188.4 33.7 %all-to-all-start.4 = ((f32[64,512,3,4]{1,3,2,0:T(4,128)}), f32[64,512,3,4]{1,3,2,0:T(4,128)S(1)}, u32[]{:S(2)}, u32[]{:S(2)}) async-start(f32[64,512,3,4]{1,3,2,0:T(4,128)} %copy.64), calls=%async_computation.4 | async-start | bytes 3145728 | tf_op jit(solution)/shard_map/all_to_all | solution.py:17
  223.0 16.4 %all-to-all-start.5 = ((f32[4,512,3,1,4]{1,4,2,3,0:T(4,128)}), f32[4,512,3,1,4]{1,4,2,3,0:T(4,128)S(1)}, u32[]{:S(2)}, u32[]{:S(2)}) async-start(f32[4,512,3,1,4]{1,4,2,3,0:T(4,128)} %broadcast_in_dim.20), calls=%async_computation.5 | async-start | bytes 196608 | tf_op jit(solution)/shard_map/all_to_all | solution.py:23
where the time goes:
time: 242 us; the launch traced here: 241 us
  waiting for transfers between devices  83.9 us (35%)
  local copies, waits for them, and re-layouts  68.4 us (28%)
  starting transfers between devices  39.7 us (16%)
  blocking collectives  28.6 us (12%)
  matrix products  14.3 us (6%)
  other arithmetic  4.98 us (2%)
    all_to_all x2, waiting for transfers between devices, copy_for_each(): lax.all_to_all(jnp.broadcast_to(value[None], (length, *value.shape)), axi...  42.1 us
    unnamed x17, local copies, waits for them, and re-layouts  30 us
    all_to_all x1, waiting for transfers between devices, summed_on_arrival(): lax.all_to_all(tiles, axis, split_axis=0, concat_axis=0, tiled=True)  27 us
    all_to_all x2, starting transfers between devices, copy_for_each(): lax.all_to_all(jnp.broadcast_to(value[None], (length, *value.shape)), axi...  25.7 us
    all_to_all x1, blocking collectives, shards(): lax.all_to_all(results, 'seq', split_axis=0, concat_axis=2, tiled=True)  19.7 us
    all_to_all x1, waiting for transfers between devices, shards(): lax.all_to_all(stacked, 'seq', split_axis=2, concat_axis=0, tiled=True)  14.8 us
    all_to_all x2, local copies, waits for them, and re-layouts, shards(): lax.all_to_all(results, 'seq', split_axis=0, concat_axis=2, tiled=True)  12.2 us
    div x2, local copies, waits for them, and re-layouts, local_convolve(): result = result.reshape(total, branch_count * narrow)[:length] / total  10.8 us
  transfers between devices with their start and end apart: 4, of which 4 were waited for; matrix products, arithmetic and copies ran while one was open for 1% of the time, Pallas kernels for 0%

commit v1 on v0

--- a/solution.py
+++ b/solution.py
@@ -5,6 +5,15 @@
 from jax.sharding import PartitionSpec as P
 
 precise_mode = lax.Precision.HIGHEST
+
+
+def panels_find(local):
+    return jnp.concatenate(
+        lax.all_to_all(
+            jnp.stack(jnp.split(local, lax.axis_size("seq"), axis=0), axis=0), "seq", 0, 0
+        ),
+        2,
+    )
 
 
 def in_blocks(value, dim, length):
@@ -152,7 +161,7 @@
     stacked = jnp.stack([filters, inner, upstream], axis=1)
     whole_length = lax.all_to_all(stacked, "seq", split_axis=2, concat_axis=0, tiled=True)
     results = local_convolve(whole_length)
-    returned = lax.all_to_all(results, "seq", split_axis=0, concat_axis=2, tiled=True)
+    returned = panels_find(results)
     conv = returned[:, 0]
     grad_inner = returned[:, 1]
     filter_raw = returned[:, 2]

time: 242 us -> 190 us (0.79)
  local copies, waits for them, and re-layouts: 68.4 us -> 18.7 us
    unnamed x17 -> x78, local copies, waits for them, and re-layouts: 30 us -> 2.99 us
    all_to_all x2 -> x0, local copies, waits for them, and re-layouts: 12.2 us -> none  [shards(): lax.all_to_all(results, 'seq', split_axis=0, concat_axis=2, tiled=True)]
    div x2 -> x0, local copies, waits for them, and re-layouts: 10.8 us -> none  [local_convolve(): result = result.reshape(total, branch_count * narrow)[:length] / total]
where the time goes in v1:
time: 190 us
  waiting for transfers between devices  83.9 us (44%)
  starting transfers between devices  39.7 us (21%)
  blocking collectives  28.6 us (15%)
  local copies, waits for them, and re-layouts  18.7 us (10%)
  matrix products  14.3 us (8%)
  other arithmetic  3.41 us (2%)
    all_to_all x2, waiting for transfers between devices, copy_for_each(): lax.all_to_all(jnp.broadcast_to(value[None], (length, *value.shape)), axi...  42.1 us
    all_to_all x1, waiting for transfers between devices, summed_on_arrival(): lax.all_to_all(tiles, axis, split_axis=0, concat_axis=0, tiled=True)  27 us
    all_to_all x2, starting transfers between devices, copy_for_each(): lax.all_to_all(jnp.broadcast_to(value[None], (length, *value.shape)), axi...  25.7 us
    all_to_all x1, blocking collectives, panels_find(): lax.all_to_all(jnp.stack(jnp.split(local, lax.axis_size('seq'), axis=0),...  19.7 us
    all_to_all x1, waiting for transfers between devices, shards(): lax.all_to_all(stacked, 'seq', split_axis=2, concat_axis=0, tiled=True)  14.8 us
    all_to_all x1, blocking collectives, summed_on_arrival(): lax.all_to_all(tiles, axis, split_axis=0, concat_axis=0, tiled=True)  8.96 us
    all_to_all x1, starting transfers between devices, shards(): lax.all_to_all(stacked, 'seq', split_axis=2, concat_axis=0, tiled=True)  8.64 us
    all_to_all x1, starting transfers between devices, summed_on_arrival(): lax.all_to_all(tiles, axis, split_axis=0, concat_axis=0, tiled=True)  5.29 us
  transfers between devices with their start and end apart: 4, of which 4 were waited for; matrix products, arithmetic and copies ran while one was open for 1% of the time, Pallas kernels for 0%

profile of v1, /device:TPU:1, one launch (start us, length us, event | category | flops | bytes accessed | tf_op | source)
XLA Modules:
  0.0 189.9 jit_solution(4155411068539028775)
XLA Ops:
  2.4 9.0 %all_to_all.40 = f32[4,512,3,1,4]{1,4,2,3,0:T(4,128)S(1)} all-to-all(f32[4,512,3,1,4]{1,4,2,3,0:T(4,128)S(1)} %copy.177), channel_id=1, replica_groups=mesh['seq'=64,'red'=4] {'red'}, dimensions={0} | all-to-all | bytes 196608 | tf_op jit(solution)/shard_map/all_to_all | solution.py:26
  11.4 1.4 broadcast_in_dim.17
  12.8 12.7 %all-to-all-start.1 = ((f32[64,512,3,1,4]{1,4,2,3,0:T(4,128)}), f32[64,512,3,1,4]{1,4,2,3,0:T(4,128)S(1)}, u32[]{:S(2)}, u32[]{:S(2)}) async-start(f32[64,512,3,1,4]{1,4,2,3,0:T(4,128)} %broadcast_in_dim.17), calls=%async_computation.1 | async-start | bytes 3145728 | tf_op jit(solution)/shard_map/all_to_all | solution.py:32
  25.6 39.4 %all-to-all-done.1 = f32[64,512,3,1,4]{1,4,2,3,0:T(4,128)S(1)} async-done(((f32[64,512,3,1,4]{1,4,2,3,0:T(4,128)}), f32[64,512,3,1,4]{1,4,2,3,0:T(4,128)S(1)}, u32[]{:S(2)}, u32[]{:S(2)}) %all-to-all-start.1) | async-done | bytes 1572896 | tf_op jit(solution)/shard_map/all_to_all | solution.py:32
  65.0 1.5 copy.178
  66.5 1.8 reshape.386
  68.3 1.8 copy.179
  70.1 2.5 %gather_fusion = f32[128,3,256]{2,1,0:T(4,128)S(1)} fusion(f32[512,3,256]{2,1,0:T(4,128)} %copy.179, s32[1024]{0:T(1024)S(1)} %pad_clamp_fusion), kind=kCustom, calls=%fused_computation | custom fusion | bytes 786944 | tf_op jit(solution)/shard_map/jit(_take)/gather | solution.py:154
  73.6 1.0 copy.181
  74.6 8.6 %all-to-all-start.2 = ((f32[128,3,256]{0,1,2:T(4,128)}), f32[128,3,256]{0,1,2:T(4,128)S(1)}, u32[]{:S(2)}, u32[]{:S(2)}) async-start(f32[128,3,256]{0,1,2:T(4,128)} %copy.181), calls=%async_computation.2 | async-start | bytes 1048576 | tf_op jit(solution)/shard_map/all_to_all | solution.py:162
  83.9 14.8 %all-to-all-done.2 = f32[128,3,256]{0,1,2:T(4,128)S(1)} async-done(((f32[128,3,256]{0,1,2:T(4,128)}), f32[128,3,256]{0,1,2:T(4,128)S(1)}, u32[]{:S(2)}, u32[]{:S(2)}) %all-to-all-start.2) | async-done | bytes 393248 | tf_op jit(solution)/shard_map/all_to_all | solution.py:162
  99.4 1.1 fusion.4
  100.5 1.1 fusion.6
  102.6 1.0 fusion.31
  103.6 1.0 fusion.1
  104.7 1.0 fusion
  110.1 1.3 fusion.10
  111.4 1.1 fusion.8
  113.6 19.7 %all_to_all.41 = f32[64,128,3,4]{1,3,2,0:T(4,128)S(1)} all-to-all(f32[64,128,3,4]{1,3,2,0:T(4,128)S(1)} %constant_dynamic-update-slice_fusion), channel_id=1, replica_groups=mesh['seq'=64,'red'=4] {'seq'}, dimensions={0} | all-to-all | bytes 786432 | tf_op jit(solution)/shard_map/all_to_all | solution.py:12
  135.2 2.2 %copy.190 = f32[64,512,3,4]{1,3,2,0:T(4,128)} copy(f32[64,512,3,4]{1,0,3,2:T(8,128)S(1)} %convolution_bitcast_fusion) | data formatting | bytes 3145728 | tf_op jit(solution)/shard_map/transpose | solution.py:21
  137.4 5.3 %all-to-all-start.4 = ((f32[64,512,3,4]{1,3,2,0:T(4,128)}), f32[64,512,3,4]{1,3,2,0:T(4,128)S(1)}, u32[]{:S(2)}, u32[]{:S(2)}) async-start(f32[64,512,3,4]{1,3,2,0:T(4,128)} %copy.190), calls=%async_computation.4 | async-start | bytes 3145728 | tf_op jit(solution)/shard_map/all_to_all | solution.py:26
  144.2 27.0 %all-to-all-done.4 = f32[64,512,3,4]{1,3,2,0:T(4,128)S(1)} async-done(((f32[64,512,3,4]{1,3,2,0:T(4,128)}), f32[64,512,3,4]{1,3,2,0:T(4,128)S(1)}, u32[]{:S(2)}, u32[]{:S(2)}) %all-to-all-start.4) | async-done | bytes 1572896 | tf_op jit(solution)/shard_map/all_to_all | solution.py:26
  172.0 13.0 %all-to-all-start.5 = ((f32[4,512,3,1,4]{1,4,2,3,0:T(4,128)}), f32[4,512,3,1,4]{1,4,2,3,0:T(4,128)S(1)}, u32[]{:S(2)}, u32[]{:S(2)}) async-start(f32[4,512,3,1,4]{1,4,2,3,0:T(4,128)} %broadcast_in_dim.20), calls=%async_computation.5 | async-start | bytes 196608 | tf_op jit(solution)/shard_map/all_to_all | solution.py:32
  185.8 2.7 %all-to-all-done.5 = f32[4,512,3,1,4]{1,4,2,3,0:T(4,128)S(1)} async-done(((f32[4,512,3,1,4]{1,4,2,3,0:T(4,128)}), f32[4,512,3,1,4]{1,4,2,3,0:T(4,128)S(1)}, u32[]{:S(2)}, u32[]{:S(2)}) %all-to-all-start.5) | async-done | bytes 98336 | tf_op jit(solution)/shard_map/all_to_all | solution.py:32
  (125 shorter events, 16.5 us)
Async XLA Ops:
  0.6 1.3 copy-start
  12.7 12.7 %copy-start.2 = (f32[128,256]{1,0:T(8,128)S(1)}, f32[128,256]{1,0:T(8,128)}, u32[]{:S(2)}) copy-start(f32[128,256]{1,0:T(8,128)} %param.8) | copy-start | bytes 393220
  12.8 12.8 %copy-start.3 = (s32[128]{0:T(128)S(1)}, s32[128]{0:T(128)}, u32[]{:S(2)}) copy-start(s32[128]{0:T(128)} %param.5) | copy-start | bytes 1540
  12.8 52.2 %all-to-all-start.1 = ((f32[64,512,3,1,4]{1,4,2,3,0:T(4,128)}), f32[64,512,3,1,4]{1,4,2,3,0:T(4,128)S(1)}, u32[]{:S(2)}, u32[]{:S(2)}) async-start(f32[64,512,3,1,4]{1,4,2,3,0:T(4,128)} %broadcast_in_dim.17), calls=%async_computation.1 | async-start | bytes 3145728 | tf_op jit(solution)/shard_map/all_to_all | solution.py:32
  70.1 3.0 %copy-start.1 = (f32[128,256]{1,0:T(8,128)S(1)}, f32[128,256]{1,0:T(8,128)}, u32[]{:S(2)}) copy-start(f32[128,256]{1,0:T(8,128)} %param.9) | copy-start | bytes 393220
  74.6 24.1 %all-to-all-start.2 = ((f32[128,3,256]{0,1,2:T(4,128)}), f32[128,3,256]{0,1,2:T(4,128)S(1)}, u32[]{:S(2)}, u32[]{:S(2)}) async-start(f32[128,3,256]{0,1,2:T(4,128)} %copy.181), calls=%async_computation.2 | async-start | bytes 1048576 | tf_op jit(solution)/shard_map/all_to_all | solution.py:162
  137.4 33.7 %all-to-all-start.4 = ((f32[64,512,3,4]{1,3,2,0:T(4,128)}), f32[64,512,3,4]{1,3,2,0:T(4,128)S(1)}, u32[]{:S(2)}, u32[]{:S(2)}) async-start(f32[64,512,3,4]{1,3,2,0:T(4,128)} %copy.190), calls=%async_computation.4 | async-start | bytes 3145728 | tf_op jit(solution)/shard_map/all_to_all | solution.py:26
  172.0 16.4 %all-to-all-start.5 = ((f32[4,512,3,1,4]{1,4,2,3,0:T(4,128)}), f32[4,512,3,1,4]{1,4,2,3,0:T(4,128)S(1)}, u32[]{:S(2)}, u32[]{:S(2)}) async-start(f32[4,512,3,1,4]{1,4,2,3,0:T(4,128)} %broadcast_in_dim.20), calls=%async_computation.5 | async-start | bytes 196608 | tf_op jit(solution)/shard_map/all_to_all | solution.py:32
